TPU v7x, 128 devices: a whole 4x4x4 slice. The times are simulated.
128 devices in a mesh: row: 16 (over y, x), col: 8 (over z, core).
Axes of the slice: x: 4, y: 4, z: 4, core: 2. Of those that a mesh axis runs over, the one named last changes fastest.
Arguments:
- inputs: bfloat16 [1024, 8192], P('col', 'row'), may hold values from -6 to 6
- out_grad: bfloat16 [1024, 8192], P('col', 'row'), may hold values from -1.5 to 1.5
- gate_pre: bfloat16 [1024, 14336], P('row', 'col'), may hold values from -9 to 9
- up_pre: bfloat16 [1024, 14336], P('row', 'col'), may hold values from -6 to 6
- gate_weight: bfloat16 [8192, 14336], P('row', 'col'), may hold values from -0.0625 to 0.0625
- up_weight: bfloat16 [8192, 14336], P('row', 'col'), may hold values from -0.0625 to 0.0625
- down_weight: bfloat16 [14336, 8192], P('col', 'row'), may hold values from -0.046875 to 0.046875
Outputs:
- input_grad: float32 [1024, 8192], P('col', 'row')
- gate_grad: float32 [8192, 14336], P('row', 'col')
- up_grad: float32 [8192, 14336], P('row', 'col')
- down_grad: float32 [14336, 8192], P('col', 'row')
All inputs are finite; a program needn't handle non-finite values.
Results may differ from a plain program's by a relative error of at most 0.0029.
Values may be sent and summed in bfloat16 or wider, within the bound.
A program may use at most 128 MiB of HBM per device.

v0:
```python
import jax
import jax.numpy as jnp
from jax import lax
from jax.sharding import PartitionSpec as P

LEAD_DIMS = (((0,), (0,)), ((), ()))
LAST_DIMS = (((1,), (1,)), ((), ()))


def body(inputs, out_grad, gate_pre, up_pre, gate_weight, up_weight, down_weight):
    gate_val = gate_pre.astype(jnp.float32)
    up_val = up_pre.astype(jnp.float32)
    gate_sig = jax.nn.sigmoid(gate_val)
    hidden = (gate_val * gate_sig * up_val).astype(jnp.bfloat16)
    grad_full = lax.all_gather(out_grad, "col", axis=0, tiled=True)
    hidden_all = lax.all_gather(hidden, "row", axis=0, tiled=True)
    partial_sum = lax.dot_general(
        grad_full, down_weight, LAST_DIMS, preferred_element_type=jnp.float32
    )
    grad_hidden = lax.psum_scatter(partial_sum, "row", scatter_dimension=0, tiled=True)
    input_full = lax.all_gather(inputs, "col", axis=0, tiled=True)
    grad_gate = (grad_hidden * up_val * gate_sig * (1.0 + gate_val * (1.0 - gate_sig))).astype(
        jnp.bfloat16
    )
    grad_up = (grad_hidden * gate_val * gate_sig).astype(jnp.bfloat16)
    down_grad = lax.dot_general(
        hidden_all, grad_full, LEAD_DIMS, preferred_element_type=jnp.float32
    )
    gate_all = lax.all_gather(grad_gate, "row", axis=0, tiled=True)
    up_all = lax.all_gather(grad_up, "row", axis=0, tiled=True)
    total = lax.dot_general(gate_all, gate_weight, LAST_DIMS, preferred_element_type=jnp.float32)
    input_grad = lax.psum_scatter(
        total + lax.dot_general(up_all, up_weight, LAST_DIMS, preferred_element_type=jnp.float32),
        "col",
        scatter_dimension=0,
        tiled=True,
    )
    gate_grad = lax.dot_general(input_full, gate_all, LEAD_DIMS, preferred_element_type=jnp.float32)
    up_grad = lax.dot_general(input_full, up_all, LEAD_DIMS, preferred_element_type=jnp.float32)
    return (input_grad, gate_grad, up_grad, down_grad)


def solution(mesh):
    in_specs = (
        P("col", "row"),
        P("col", "row"),
        P("row", "col"),
        P("row", "col"),
        P("row", "col"),
        P("row", "col"),
        P("col", "row"),
    )
    out_specs = (P("col", "row"), P("row", "col"), P("row", "col"), P("col", "row"))
    return jax.shard_map(body, mesh=mesh, in_specs=in_specs, out_specs=out_specs, check_vma=False)
```

profile of v0, /device:TPU:0, one launch (start us, length us, event | category | flops | bytes accessed | tf_op | source)
XLA Modules:
  0.0 347.5 jit_solution(18138531377756682958)
XLA Ops:
  7.2 0.7 all-gather.6.cloned.1.call-update
  7.9 0.0 reduce-scatter.3.cloned.1.call-start
  8.0 27.8 %all-gather.6.cloned.1.call-done = bf16[1024,512]{1,0:T(8,128)(2,1)} async-done(((bf16[128,512]{1,0:T(8,128)(2,1)}), bf16[1024,512]{1,0:T(8,128)(2,1)}) %all-gather.6.cloned.1.call-update) | async-done | bytes 1048592 | tf_op jit(solution)/shard_map/all_gather | solution.py:15
  35.8 6.3 %fusion.10 = f32[1024,1792]{1,0:T(8,128)} fusion(bf16[1024,512]{1,0:T(8,128)(2,1)} %all-gather.6.cloned.1.call-done, bf16[1792,512]{1,0:T(8,128)(2,1)S(1)} %copy-done), kind=kOutput, calls=%fused_computation.19 | convolution fusion | flops 1879048192 | bytes 10223616 | tf_op jit(solution)/shard_map/dot_general | solution.py:17
  42.1 0.0 all-gather.8.cloned.1.call-start
  42.2 82.8 %reduce-scatter.3.cloned.1.call-done = f32[64,1792]{1,0:T(8,128)} async-done(((f32[1024,1792]{1,0:T(8,128)}), f32[64,1792]{1,0:T(8,128)}) %reduce-scatter.3.cloned.1.call-update) | async-done | bytes 458768 | tf_op jit(solution)/shard_map/reduce_scatter | solution.py:20
  124.9 2.1 fusion.9
  127.0 0.0 all-gather.10.cloned.1.call-start
  127.1 0.5 all-gather.10.cloned.1.call-update
  127.7 0.5 all-gather.12.cloned.1.call-update
  128.2 0.5 all-gather.14.cloned.1.call-update
  128.8 0.0 reduce-scatter.5.cloned.1.call-start
  128.8 47.9 %all-gather.8.cloned.1.call-done = bf16[1024,1792]{1,0:T(8,128)(2,1)} async-done(((bf16[64,1792]{1,0:T(8,128)(2,1)}), bf16[1024,1792]{1,0:T(8,128)(2,1)}) %all-gather.8.cloned.1.call-update) | async-done | bytes 3670032 | tf_op jit(solution)/shard_map/all_gather | solution.py:29
  176.7 6.0 %fusion.11 = f32[1024,512]{1,0:T(8,128)} fusion(bf16[1024,1792]{1,0:T(8,128)(2,1)} %all-gather.8.cloned.1.call-done, bf16[512,1792]{1,0:T(8,128)(2,1)} %param.11), kind=kOutput, calls=%fused_computation.20 | convolution fusion | flops 1879048192 | bytes 7602176 | tf_op jit(solution)/shard_map/dot_general | solution.py:31
  182.8 45.6 %all-gather.10.cloned.1.call-done = bf16[1024,1792]{1,0:T(8,128)(2,1)} async-done(((bf16[64,1792]{1,0:T(8,128)(2,1)}), bf16[1024,1792]{1,0:T(8,128)(2,1)}) %all-gather.10.cloned.1.call-update) | async-done | bytes 3670032 | tf_op jit(solution)/shard_map/all_gather | solution.py:30
  228.3 6.7 %convolution_add_fusion = f32[1024,512]{1,0:T(8,128)} fusion(f32[1024,512]{1,0:T(8,128)} %fusion.11, bf16[1024,1792]{1,0:T(8,128)(2,1)} %all-gather.10.cloned.1.call-done, bf16[512,1792]{1,0:T(8,128)(2,1)} %param.12), kind=kOutput, calls=%fused_computation.2 | convolution fusion | flops 1879572480 | bytes 9699328 | tf_op jit(solution)/shard_map/dot_general | solution.py:33
  235.1 17.7 %all-gather.12.cloned.1.call-done = bf16[1024,512]{1,0:T(8,128)(2,1)} async-done(((bf16[128,512]{1,0:T(8,128)(2,1)}), bf16[1024,512]{1,0:T(8,128)(2,1)}) %all-gather.12.cloned.1.call-update) | async-done | bytes 1048592 | tf_op jit(solution)/shard_map/all_gather | solution.py:21
  252.8 6.3 %convolution_bitcast_fusion.1 = f32[512,1792]{0,1:T(8,128)} fusion(bf16[1024,1792]{1,0:T(8,128)(2,1)} %all-gather.8.cloned.1.call-done, bf16[1024,512]{1,0:T(8,128)(2,1)} %all-gather.12.cloned.1.call-done), kind=kOutput, calls=%fused_computation.1 | convolution fusion | flops 1879048192 | bytes 8388608 | tf_op jit(solution)/shard_map/dot_general | solution.py:38
  259.1 5.2 %copy.11 = f32[512,1792]{1,0:T(8,128)} copy(f32[512,1792]{0,1:T(8,128)} %convolution_bitcast_fusion.1) | data formatting | bytes 7340032
  264.3 6.1 %convolution_bitcast_fusion = f32[512,1792]{0,1:T(8,128)} fusion(bf16[1024,1792]{1,0:T(8,128)(2,1)} %all-gather.10.cloned.1.call-done, bf16[1024,512]{1,0:T(8,128)(2,1)S(1)} %copy-done.4), kind=kOutput, calls=%fused_computation | convolution fusion | flops 1879048192 | bytes 8388608 | tf_op jit(solution)/shard_map/dot_general | solution.py:39
  270.4 5.2 %copy.12 = f32[512,1792]{1,0:T(8,128)} copy(f32[512,1792]{0,1:T(8,128)} %convolution_bitcast_fusion) | data formatting | bytes 7340032
  275.7 28.9 %all-gather.14.cloned.1.call-done = bf16[1024,1792]{1,0:T(8,128)(2,1)} async-done(((bf16[64,1792]{1,0:T(8,128)(2,1)}), bf16[1024,1792]{1,0:T(8,128)(2,1)}) %all-gather.14.cloned.1.call-update) | async-done | bytes 3670032 | tf_op jit(solution)/shard_map/all_gather | solution.py:16
  304.5 6.0 %fusion.12 = f32[1792,512]{1,0:T(8,128)} fusion(bf16[1024,1792]{1,0:T(8,128)(2,1)} %all-gather.14.cloned.1.call-done, bf16[1024,512]{1,0:T(8,128)(2,1)S(1)} %copy-done.3), kind=kOutput, calls=%fused_computation.21 | convolution fusion | flops 1879048192 | bytes 8388608 | tf_op jit(solution)/shard_map/dot_general | solution.py:26
  310.5 30.2 %reduce-scatter.5.cloned.1.call-done = f32[128,512]{1,0:T(8,128)} async-done(((f32[1024,512]{1,0:T(8,128)}), f32[128,512]{1,0:T(8,128)}) %reduce-scatter.5.cloned.1.call-update) | async-done | bytes 262160 | tf_op jit(solution)/shard_map/reduce_scatter | solution.py:32
  (16 shorter events, 0.2 us)
Async XLA Ops:
  7.2 28.6 %copy-start = (bf16[1792,512]{1,0:T(8,128)(2,1)S(1)}, bf16[1792,512]{1,0:T(8,128)(2,1)}, u32[]{:S(2)}) copy-start(bf16[1792,512]{1,0:T(8,128)(2,1)} %param.13) | copy-start | bytes 5505028
  7.2 28.6 %all-gather.6.cloned.1.call-start = ((), (), s32[]{:S(2)}) async-start(), calls=%async_computation.2 | async-start | bytes 1179648 | tf_op jit(solution)/shard_map/all_gather | solution.py:15
  7.9 117.0 %reduce-scatter.3.cloned.1.call-start = ((), (), s32[]{:S(2)}) async-start(), calls=%async_computation.3 | async-start | bytes 7798784 | tf_op jit(solution)/shard_map/reduce_scatter | solution.py:20
  42.1 82.8 %copy-start.1 = (bf16[64,1792]{1,0:T(8,128)(2,1)S(1)}, bf16[64,1792]{1,0:T(8,128)(2,1)}, u32[]{:S(2)}) copy-start(bf16[64,1792]{1,0:T(8,128)(2,1)} %param.9) | copy-start | bytes 688132
  42.1 82.8 %copy-start.2 = (bf16[64,1792]{1,0:T(8,128)(2,1)S(1)}, bf16[64,1792]{1,0:T(8,128)(2,1)}, u32[]{:S(2)}) copy-start(bf16[64,1792]{1,0:T(8,128)(2,1)} %param.10) | copy-start | bytes 688132
  42.1 134.6 %all-gather.8.cloned.1.call-start = ((), (), s32[]{:S(2)}) async-start(), calls=%async_computation.4 | async-start | bytes 3899392 | tf_op jit(solution)/shard_map/all_gather | solution.py:29
  127.0 101.3 %all-gather.10.cloned.1.call-start = ((), (), s32[]{:S(2)}) async-start(), calls=%async_computation.5 | async-start | bytes 3899392 | tf_op jit(solution)/shard_map/all_gather | solution.py:30
  127.6 125.2 %all-gather.12.cloned.1.call-start = ((), (), s32[]{:S(2)}) async-start(), calls=%async_computation.7 | async-start | bytes 1179648 | tf_op jit(solution)/shard_map/all_gather | solution.py:21
  128.2 176.3 %all-gather.14.cloned.1.call-start = ((), (), s32[]{:S(2)}) async-start(), calls=%async_computation.8 | async-start | bytes 3899392 | tf_op jit(solution)/shard_map/all_gather | solution.py:16
  128.8 211.9 %reduce-scatter.5.cloned.1.call-start = ((), (), s32[]{:S(2)}) async-start(), calls=%async_computation.6 | async-start | bytes 2359296 | tf_op jit(solution)/shard_map/reduce_scatter | solution.py:32
  259.1 5.2 %copy-start.4 = (bf16[1024,512]{1,0:T(8,128)(2,1)S(1)}, bf16[1024,512]{1,0:T(8,128)(2,1)}, u32[]{:S(2)}) copy-start(bf16[1024,512]{1,0:T(8,128)(2,1)} %all-gather.12.cloned.1.call-done) | copy-start | bytes 3145732
  270.4 34.1 %copy-start.3 = (bf16[1024,512]{1,0:T(8,128)(2,1)S(1)}, bf16[1024,512]{1,0:T(8,128)(2,1)}, u32[]{:S(2)}) copy-start(bf16[1024,512]{1,0:T(8,128)(2,1)} %all-gather.6.cloned.1.call-done) | copy-start | bytes 3145732
Sparse Core Ops, SparseCore 0:
  9.7 26.0 all-gather.5
  42.2 82.6 reduce-scatter.2
  127.9 48.8 all-gather.7
  179.5 48.7 all-gather.9
  230.0 22.7 all-gather.11
  255.1 49.4 all-gather.13
  307.6 32.9 reduce-scatter.4
where the time goes:
time: 348 us; the launch traced here: 347 us
  waiting for transfers between devices  283 us (81%)
  matrix products  37.4 us (11%)
  between operations  14.1 us (4%)
  local copies, waits for them, and re-layouts  10.5 us (3%)
    reduce_scatter x1, waiting for transfers between devices, body(): lax.psum_scatter(partial_sum, 'row', scatter_dimension=0, tiled=True)  82.8 us
    all_gather x1, waiting for transfers between devices, body(): gate_all = lax.all_gather(grad_gate, 'row', axis=0, tiled=True)  47.9 us
    all_gather x1, waiting for transfers between devices, body(): up_all = lax.all_gather(grad_up, 'row', axis=0, tiled=True)  45.6 us
    reduce_scatter x1, waiting for transfers between devices, body(): lax.psum_scatter(total + lax.dot_general(up_all, up_weight, LAST_DIMS, pr...  30.2 us
    all_gather x1, waiting for transfers between devices, body(): hidden_all = lax.all_gather(hidden, 'row', axis=0, tiled=True)  28.9 us
    all_gather x1, waiting for transfers between devices, body(): grad_full = lax.all_gather(out_grad, 'col', axis=0, tiled=True)  27.8 us
    all_gather x1, waiting for transfers between devices, body(): input_full = lax.all_gather(inputs, 'col', axis=0, tiled=True)  17.7 us
    unnamed x12, local copies, waits for them, and re-layouts  10.5 us
  transfers between devices with their start and end apart: 7, of which 7 were waited for; matrix products, arithmetic and copies ran while one was open for 12% of the time, Pallas kernels for 0%

commit v1 on v0

--- a/solution.py
+++ b/solution.py
@@ -26,7 +26,9 @@
     down_grad = lax.dot_general(
         hidden_all, grad_full, LEAD_DIMS, preferred_element_type=jnp.float32
     )
-    gate_all = lax.all_gather(grad_gate, "row", axis=0, tiled=True)
+    gate_all = jnp.concatenate(
+        lax.all_to_all(jnp.stack([grad_gate] * lax.axis_size("row")), "row", 0, 0), axis=0
+    )
     up_all = lax.all_gather(grad_up, "row", axis=0, tiled=True)
     total = lax.dot_general(gate_all, gate_weight, LAST_DIMS, preferred_element_type=jnp.float32)
     input_grad = lax.psum_scatter(

time: 348 us -> 319 us (0.917)
  waiting for transfers between devices: 283 us -> 201 us
  blocking collectives: 0 us -> 53.5 us
    all_to_all x0 -> x1, blocking collectives: none -> 53.5 us  [body(): lax.all_to_all(jnp.stack([grad_gate] * lax.axis_size('row')), 'row', 0, 0)]
    all_gather x1 -> x0, waiting for transfers between devices: 47.9 us -> none  [body(): gate_all = lax.all_gather(grad_gate, 'row', axis=0, tiled=True)]
    all_gather x1, waiting for transfers between devices: 45.6 us -> 12.2 us  [body(): up_all = lax.all_gather(grad_up, 'row', axis=0, tiled=True)]
    unnamed x12 -> x16, local copies, waits for them, and re-layouts: 10.5 us -> 12.3 us
  transfers between devices with their start and end apart: 7 -> 6, of which waited for: 7 -> 6; matrix products, arithmetic and copies ran while one was open for 12% -> 12% of each run, Pallas kernels for 0% -> 0%
where the time goes in v1:
time: 319 us
  waiting for transfers between devices  201 us (63%)
  blocking collectives  53.5 us (17%)
  matrix products  34.8 us (11%)
  between operations  14.1 us (4%)
  local copies, waits for them, and re-layouts  12.7 us (4%)
    reduce_scatter x1, waiting for transfers between devices, body(): lax.psum_scatter(partial_sum, 'row', scatter_dimension=0, tiled=True)  82.8 us
    all_to_all x1, blocking collectives, body(): lax.all_to_all(jnp.stack([grad_gate] * lax.axis_size('row')), 'row', 0, 0)  53.5 us
    reduce_scatter x1, waiting for transfers between devices, body(): lax.psum_scatter(total + lax.dot_general(up_all, up_weight, LAST_DIMS, pr...  30 us
    all_gather x1, waiting for transfers between devices, body(): hidden_all = lax.all_gather(hidden, 'row', axis=0, tiled=True)  28.9 us
    all_gather x1, waiting for transfers between devices, body(): grad_full = lax.all_gather(out_grad, 'col', axis=0, tiled=True)  27.8 us
    all_gather x1, waiting for transfers between devices, body(): input_full = lax.all_gather(inputs, 'col', axis=0, tiled=True)  17.8 us
    unnamed x16, local copies, waits for them, and re-layouts  12.3 us
    all_gather x1, waiting for transfers between devices, body(): up_all = lax.all_gather(grad_up, 'row', axis=0, tiled=True)  12.2 us
  transfers between devices with their start and end apart: 6, of which 6 were waited for; matrix products, arithmetic and copies ran while one was open for 12% of the time, Pallas kernels for 0%

profile of v1, /device:TPU:0, one launch (start us, length us, event | category | flops | bytes accessed | tf_op | source)
XLA Modules:
  0.0 318.6 jit_solution(1621211691455223189)
XLA Ops:
  7.2 0.7 all-gather.5.cloned.1.call-update
  8.0 27.8 %all-gather.5.cloned.1.call-done = bf16[1024,512]{1,0:T(8,128)(2,1)} async-done(((bf16[128,512]{1,0:T(8,128)(2,1)}), bf16[1024,512]{1,0:T(8,128)(2,1)}) %all-gather.5.cloned.1.call-update) | async-done | bytes 1048592 | tf_op jit(solution)/shard_map/all_gather | solution.py:15
  35.8 6.3 %fusion.10 = f32[1024,1792]{1,0:T(8,128)} fusion(bf16[1024,512]{1,0:T(8,128)(2,1)} %all-gather.5.cloned.1.call-done, bf16[1792,512]{1,0:T(8,128)(2,1)S(1)} %copy-done), kind=kOutput, calls=%fused_computation.19 | convolution fusion | flops 1879048192 | bytes 10223616 | tf_op jit(solution)/shard_map/dot_general | solution.py:17
  42.1 0.0 all-gather.7.cloned.1.call-start
  42.2 82.8 %reduce-scatter.3.cloned.1.call-done = f32[64,1792]{1,0:T(8,128)} async-done(((f32[1024,1792]{1,0:T(8,128)}), f32[64,1792]{1,0:T(8,128)}) %reduce-scatter.3.cloned.1.call-update) | async-done | bytes 458768 | tf_op jit(solution)/shard_map/reduce_scatter | solution.py:20
  124.9 2.1 fusion.9
  127.0 0.0 all-gather.9.cloned.1.call-start
  127.1 0.5 all-gather.9.cloned.1.call-update
  127.6 0.5 all-gather.11.cloned.1.call-update
  128.2 0.0 reduce-scatter.5.cloned.1.call-start
  128.2 0.4 stack.2
  128.6 53.5 %all_to_all.5 = bf16[16,64,1792]{2,1,0:T(8,128)(2,1)S(1)} all-to-all(bf16[16,64,1792]{2,1,0:T(8,128)(2,1)S(1)} %stack.2), channel_id=1, replica_groups=mesh['row'=16,'col'=8] {'row'}, dimensions={0} | all-to-all | bytes 7340032 | tf_op jit(solution)/shard_map/all_to_all | solution.py:30
  182.1 1.8 copy-done.1
  183.9 3.4 %fusion.11 = f32[1024,512]{1,0:T(8,128)} fusion(bf16[1024,1792]{1,0:T(8,128)(2,1)S(1)} %bitcast.17, bf16[512,1792]{1,0:T(8,128)(2,1)S(1)} %copy-done.4), kind=kOutput, calls=%fused_computation.20 | convolution fusion | flops 1879048192 | bytes 7602176 | tf_op jit(solution)/shard_map/dot_general | solution.py:33
  187.3 12.2 %all-gather.7.cloned.1.call-done = bf16[1024,1792]{1,0:T(8,128)(2,1)} async-done(((bf16[64,1792]{1,0:T(8,128)(2,1)}), bf16[1024,1792]{1,0:T(8,128)(2,1)}) %all-gather.7.cloned.1.call-update) | async-done | bytes 3670032 | tf_op jit(solution)/shard_map/all_gather | solution.py:32
  199.5 6.7 %convolution_add_fusion = f32[1024,512]{1,0:T(8,128)} fusion(f32[1024,512]{1,0:T(8,128)} %fusion.11, bf16[1024,1792]{1,0:T(8,128)(2,1)} %all-gather.7.cloned.1.call-done, bf16[512,1792]{1,0:T(8,128)(2,1)} %param.12), kind=kOutput, calls=%fused_computation.2 | convolution fusion | flops 1879572480 | bytes 9699328 | tf_op jit(solution)/shard_map/dot_general | solution.py:35
  206.3 17.8 %all-gather.9.cloned.1.call-done = bf16[1024,512]{1,0:T(8,128)(2,1)} async-done(((bf16[128,512]{1,0:T(8,128)(2,1)}), bf16[1024,512]{1,0:T(8,128)(2,1)}) %all-gather.9.cloned.1.call-update) | async-done | bytes 1048592 | tf_op jit(solution)/shard_map/all_gather | solution.py:21
  224.1 6.3 %convolution_bitcast_fusion.1 = f32[512,1792]{0,1:T(8,128)} fusion(bf16[1024,1792]{1,0:T(8,128)(2,1)} %bitcast.18, bf16[1024,512]{1,0:T(8,128)(2,1)} %all-gather.9.cloned.1.call-done), kind=kOutput, calls=%fused_computation.1 | convolution fusion | flops 1879048192 | bytes 8388608 | tf_op jit(solution)/shard_map/dot_general | solution.py:40
  230.3 5.2 %copy.11 = f32[512,1792]{1,0:T(8,128)} copy(f32[512,1792]{0,1:T(8,128)} %convolution_bitcast_fusion.1) | data formatting | bytes 7340032
  235.5 6.1 %convolution_bitcast_fusion = f32[512,1792]{0,1:T(8,128)} fusion(bf16[1024,1792]{1,0:T(8,128)(2,1)} %all-gather.7.cloned.1.call-done, bf16[1024,512]{1,0:T(8,128)(2,1)S(1)} %copy-done.6), kind=kOutput, calls=%fused_computation | convolution fusion | flops 1879048192 | bytes 8388608 | tf_op jit(solution)/shard_map/dot_general | solution.py:41
  241.6 5.2 %copy.12 = f32[512,1792]{1,0:T(8,128)} copy(f32[512,1792]{0,1:T(8,128)} %convolution_bitcast_fusion) | data formatting | bytes 7340032
  246.9 28.9 %all-gather.11.cloned.1.call-done = bf16[1024,1792]{1,0:T(8,128)(2,1)} async-done(((bf16[64,1792]{1,0:T(8,128)(2,1)}), bf16[1024,1792]{1,0:T(8,128)(2,1)}) %all-gather.11.cloned.1.call-update) | async-done | bytes 3670032 | tf_op jit(solution)/shard_map/all_gather | solution.py:16
  275.7 6.0 %fusion.12 = f32[1792,512]{1,0:T(8,128)} fusion(bf16[1024,1792]{1,0:T(8,128)(2,1)} %all-gather.11.cloned.1.call-done, bf16[1024,512]{1,0:T(8,128)(2,1)S(1)} %copy-done.5), kind=kOutput, calls=%fused_computation.21 | convolution fusion | flops 1879048192 | bytes 8388608 | tf_op jit(solution)/shard_map/dot_general | solution.py:26
  281.7 30.0 %reduce-scatter.5.cloned.1.call-done = f32[128,512]{1,0:T(8,128)} async-done(((f32[1024,512]{1,0:T(8,128)}), f32[128,512]{1,0:T(8,128)}) %reduce-scatter.5.cloned.1.call-update) | async-done | bytes 262160 | tf_op jit(solution)/shard_map/reduce_scatter | solution.py:34
  (19 shorter events, 0.2 us)
Async XLA Ops:
  7.2 28.6 %copy-start = (bf16[1792,512]{1,0:T(8,128)(2,1)S(1)}, bf16[1792,512]{1,0:T(8,128)(2,1)}, u32[]{:S(2)}) copy-start(bf16[1792,512]{1,0:T(8,128)(2,1)} %param.13) | copy-start | bytes 5505028
  7.2 28.6 %all-gather.5.cloned.1.call-start = ((), (), s32[]{:S(2)}) async-start(), calls=%async_computation.3 | async-start | bytes 1179648 | tf_op jit(solution)/shard_map/all_gather | solution.py:15
  7.9 117.0 %reduce-scatter.3.cloned.1.call-start = ((), (), s32[]{:S(2)}) async-start(), calls=%async_computation.4 | async-start | bytes 7798784 | tf_op jit(solution)/shard_map/reduce_scatter | solution.py:20
  42.1 82.8 %copy-start.2 = (bf16[64,1792]{1,0:T(8,128)(2,1)S(1)}, bf16[64,1792]{1,0:T(8,128)(2,1)}, u32[]{:S(2)}) copy-start(bf16[64,1792]{1,0:T(8,128)(2,1)} %param.9) | copy-start | bytes 688132
  42.1 82.8 %copy-start.3 = (bf16[64,1792]{1,0:T(8,128)(2,1)S(1)}, bf16[64,1792]{1,0:T(8,128)(2,1)}, u32[]{:S(2)}) copy-start(bf16[64,1792]{1,0:T(8,128)(2,1)} %param.10) | copy-start | bytes 688132
  42.1 157.4 %all-gather.7.cloned.1.call-start = ((), (), s32[]{:S(2)}) async-start(), calls=%async_computation.5 | async-start | bytes 3899392 | tf_op jit(solution)/shard_map/all_gather | solution.py:32
  127.0 97.0 %all-gather.9.cloned.1.call-start = ((), (), s32[]{:S(2)}) async-start(), calls=%async_computation.7 | async-start | bytes 1179648 | tf_op jit(solution)/shard_map/all_gather | solution.py:21
  127.6 148.1 %all-gather.11.cloned.1.call-start = ((), (), s32[]{:S(2)}) async-start(), calls=%async_computation.8 | async-start | bytes 3899392 | tf_op jit(solution)/shard_map/all_gather | solution.py:16
  128.2 183.5 %reduce-scatter.5.cloned.1.call-start = ((), (), s32[]{:S(2)}) async-start(), calls=%async_computation.6 | async-start | bytes 2359296 | tf_op jit(solution)/shard_map/reduce_scatter | solution.py:34
  128.6 55.3 %copy-start.4 = (bf16[512,1792]{1,0:T(8,128)(2,1)S(1)}, bf16[512,1792]{1,0:T(8,128)(2,1)}, u32[]{:S(2)}) copy-start(bf16[512,1792]{1,0:T(8,128)(2,1)} %param.11) | copy-start | bytes 5505028
  182.1 1.8 copy-start.1
  230.3 5.2 %copy-start.6 = (bf16[1024,512]{1,0:T(8,128)(2,1)S(1)}, bf16[1024,512]{1,0:T(8,128)(2,1)}, u32[]{:S(2)}) copy-start(bf16[1024,512]{1,0:T(8,128)(2,1)} %all-gather.9.cloned.1.call-done) | copy-start | bytes 3145732
  241.6 34.1 %copy-start.5 = (bf16[1024,512]{1,0:T(8,128)(2,1)S(1)}, bf16[1024,512]{1,0:T(8,128)(2,1)}, u32[]{:S(2)}) copy-start(bf16[1024,512]{1,0:T(8,128)(2,1)} %all-gather.5.cloned.1.call-done) | copy-start | bytes 3145732
Sparse Core Ops, SparseCore 0:
  9.7 26.0 all-gather.4
  42.2 82.6 reduce-scatter.2
  127.9 71.6 all-gather.6
  201.2 22.7 all-gather.8
  226.3 49.4 all-gather.10
  278.7 32.9 reduce-scatter.4
